TPU v7x, 128 devices: a whole 4x4x4 slice. The times are simulated.
128 devices in a mesh: elec: 8 (over x_hi, y), space: 16 (over z, x_lo, core).
Axes of the slice: x: 4 (x_hi: 2, x_lo: 2; x = x_hi * 2 + x_lo), y: 4, z: 4, core: 2. Of those that a mesh axis runs over, the one named last changes fastest.
Arguments:
- potentials: float32 [32, 1024, 8192], P('space', 'elec'), may hold values from -6 to 6
- measurements: int32 [16384, 4], replicated, may hold values from 0 to 1023, all different within a row
- residuals: float32 [2, 16384], replicated, may hold values from -0.03 to 0.03
- conductivity: float32 [32, 8192], P('space', 'elec'), may hold values from 0.1 to 1
- inside: int32 [32, 8192], P('space', 'elec'), may hold values 0 or 1
Outputs:
- gradient: float32 [2, 32, 8192], P(None, 'space', 'elec')
- scaled: float32 [2, 32, 8192], P(None, 'space', 'elec')
Inputs may be any that keep to these rules, and one draw needn't show every extreme that they name: `measurements`: each row names four different electrodes, in the order A, B, M, N.
All inputs are finite; a program needn't handle non-finite values. No bound on the sum of `inside` on one device may be relied on, other than what follows from the above.
Results may differ from a plain program's by a relative error of at most 0.0066.
Values may be sent and summed in bfloat16 or wider, within the bound.
A program may use at most 256 MiB of HBM per device.

v0:
```python
import functools

import jax
import jax.numpy as jnp
from jax import lax
from jax.experimental import pallas as pl
from jax.experimental.pallas import tpu as pltpu
from jax.sharding import PartitionSpec as P

ELECTRODES = 1024
NY = 128
ROWS = 4
SLAB = (ROWS + 1) * NY
OWN = ROWS * NY
MESH = pl.DeviceIdType.MESH
BF = jnp.bfloat16
F32 = jnp.float32
OFFSETS = [(2, 2), (1, 0), (0, 3), (2, 1), (3, 0), (0, 1), (1, 2), (3, 3), (2, 0), (0, 2), (1, 1), (3, 2), (2, 3), (1, 3), (3, 1)]
QUAD_CHUNK = 1024
ZCOL = 4 * SLAB


def device_of(x, y, z, c):
    return (lax.div(x, 2) * 4 + y, z * 4 + lax.rem(x, 2) * 2 + c)


def kernel_body(pot, quads, resid, cond, inside, grad_out, scaled_out,
                stage, send, field, weights, wacc, psi, sens, mine, other, totals,
                stage_sem, own_sem, out_sem, in_sem, zs_sem, zr_sem, ws_sem, wr_sem, ds_sem, dr_sem,
                ps_sem, pr_sem, ts_sem, tr_sem):
    e = lax.axis_index("elec")
    s = lax.axis_index("space")
    y = lax.rem(e, 4)
    xh = lax.div(e, 4)
    c = lax.rem(s, 2)
    xl = lax.rem(lax.div(s, 2), 2)
    z = lax.div(s, 4)
    x = xh * 2 + xl
    n_off = len(OFFSETS)

    cells = pot.shape[2]
    quarter = cells // 4

    def stage_copy(p, q):
        cols = pl.ds(q * quarter, quarter)
        return pltpu.make_async_copy(pot.at[p, :, cols], stage.at[p, :, cols], stage_sem.at[p, q])

    for p in range(2):
        for q in range(4):
            stage_copy(p, q).start()

    bar = pltpu.get_barrier_semaphore()
    for dx, dy in OFFSETS:
        pl.semaphore_signal(bar, inc=1, device_id=device_of(lax.rem(x + dx, 4), lax.rem(y + dy, 4), z, c), device_id_type=MESH)
    for i in range(1, 16):
        pl.semaphore_signal(bar, inc=1, device_id=(e, lax.rem(s + i, 16)), device_id_type=MESH)

    def slab_copy(p, i):
        dx, dy = OFFSETS[i]
        tx = lax.rem(x + dx, 4)
        ty = lax.rem(y + dy, 4)
        block = (lax.div(tx, 2) * 4 + ty) * 2 + lax.rem(tx, 2)
        return pltpu.make_async_remote_copy(
            src_ref=send.at[p, :, pl.ds(pl.multiple_of(block * OWN, OWN), SLAB)],
            dst_ref=field.at[pl.ds(pl.multiple_of(e * 128, 128), 128), pl.ds(pl.multiple_of((xl * 2 + p) * SLAB, 128), SLAB)],
            send_sem=out_sem.at[p, i], recv_sem=in_sem.at[p, i],
            device_id=device_of(tx, ty, z, c), device_id_type=MESH)

    row_block = e * 2 + xl

    def own_copy(p):
        return pltpu.make_async_copy(
            send.at[p, :, pl.ds(pl.multiple_of(row_block * OWN, OWN), SLAB)],
            field.at[pl.ds(pl.multiple_of(e * 128, 128), 128), pl.ds(pl.multiple_of((xl * 2 + p) * SLAB, 128), SLAB)],
            own_sem.at[p])

    for p in range(2):
        send[p, :, pl.ds(cells, NY)] = jnp.zeros((128, NY), BF)
        for q in range(4):
            stage_copy(p, q).wait()

            def cast(i, _):
                rows = pl.ds(pl.multiple_of(i * 16, 16), 16)
                cols = pl.ds(q * quarter, quarter)
                send[p, rows, cols] = stage[p, rows, cols].astype(BF)
                return 0
            lax.fori_loop(0, 8, cast, 0)
        if p == 0:
            pl.semaphore_wait(bar, n_off + 15)
        for i in range(n_off):
            slab_copy(p, i).start()
        own_copy(p).start()

    quarter_f = 256
    half_e = 512
    wacc[...] = jnp.zeros_like(wacc)
    f_ids = z * quarter_f + lax.broadcasted_iota(jnp.int32, (quarter_f, QUAD_CHUNK), 0)
    e_ids = c * half_e + lax.broadcasted_iota(jnp.int32, (half_e, QUAD_CHUNK), 0)

    def add_quads(i, _):
        cols = pl.ds(pl.multiple_of(i * QUAD_CHUNK, QUAD_CHUNK), QUAD_CHUNK)
        left = (jnp.where(quads[2:3, cols] == f_ids, 1.0, 0.0) - jnp.where(quads[3:4, cols] == f_ids, 1.0, 0.0)).astype(BF)
        right = (jnp.where(quads[0:1, cols] == e_ids, 1.0, 0.0) - jnp.where(quads[1:2, cols] == e_ids, 1.0, 0.0)).astype(BF)
        for k in range(2):
            r = resid[k:k + 1, cols]
            hi = r.astype(BF)
            lo = (r - hi.astype(F32)).astype(BF)
            for part in (hi, lo):
                wacc[k] += lax.dot_general(left * part, right, (((1,), (1,)), ((), ())), preferred_element_type=F32)
        return 0
    lax.fori_loop(0, quads.shape[1] // QUAD_CHUNK, add_quads, 0)

    def block_of(zz, cc):
        return weights.at[:, pl.ds(pl.multiple_of(zz * quarter_f, quarter_f), quarter_f), pl.ds(pl.multiple_of(cc * half_e, half_e), half_e)]

    weights[:, pl.ds(pl.multiple_of(z * quarter_f, quarter_f), quarter_f), pl.ds(pl.multiple_of(c * half_e, half_e), half_e)] = wacc[...].astype(BF)

    def w_copy(d):
        tz = lax.rem(z + d, 4)
        return pltpu.make_async_remote_copy(
            src_ref=block_of(z, c), dst_ref=block_of(z, c), send_sem=ws_sem.at[d], recv_sem=wr_sem.at[d],
            device_id=device_of(x, y, tz, c), device_id_type=MESH)

    def w_across(d):
        zz = lax.rem(z + 4 - d, 4)
        return pltpu.make_async_remote_copy(
            src_ref=block_of(zz, c), dst_ref=block_of(zz, c), send_sem=ds_sem.at[d], recv_sem=dr_sem.at[d],
            device_id=device_of(x, y, z, 1 - c), device_id_type=MESH)

    for d in (1, 3, 2):
        w_copy(d).start()
    w_across(0).start()

    for i in range(n_off):
        slab_copy(0, i).wait_recv()
    own_copy(0).wait()

    def halo_copy(j):
        slot = jnp.where(c == 0, 2 - 2 * j, 2 * j)
        if j == 0:
            target = device_of(x, y, z, 1 - c)
        else:
            target = device_of(x, y, jnp.where(c == 0, lax.rem(z + 3, 4), z), 1 - c)
        return pltpu.make_async_remote_copy(
            src_ref=field.at[:, pl.ds(pl.multiple_of(slot * SLAB, 128), OWN)],
            dst_ref=field.at[:, pl.ds(ZCOL + j * OWN, OWN)],
            send_sem=zs_sem.at[j], recv_sem=zr_sem.at[j], device_id=target, device_id_type=MESH)

    for j in (1, 0):
        halo_copy(j).start()

    for d in (1, 3, 2):
        w_copy(d).wait_recv()
        w_across(d).start()
    for d in (0, 1, 3, 2):
        w_across(d).wait_recv()

    def adjoint(col, width):
        def block(i, _):
            k = lax.div(i, 4)
            rows = pl.ds(pl.multiple_of(lax.rem(i, 4) * 256, 256), 256)
            cols = pl.ds(col, width)
            psi[k, rows, cols] = jnp.dot(weights[k, rows, :], field[:, cols], preferred_element_type=F32).astype(BF)
            return 0
        lax.fori_loop(0, 8, block, 0)

    adjoint(0, SLAB)
    adjoint(2 * SLAB, SLAB)

    for j in range(2):
        halo_copy(j).wait_recv()
        adjoint(ZCOL + j * OWN, OWN)

    for i in range(n_off):
        slab_copy(1, i).wait_recv()
    own_copy(1).wait()
    adjoint(SLAB, SLAB)
    adjoint(3 * SLAB, SLAB)

    lane_keep = (lax.broadcasted_iota(jnp.int32, (16, NY), 1) < NY - 1).astype(F32)
    row_keep = (row_block < 15).astype(F32)
    depth_keep = jnp.logical_or(c == 0, z < 3).astype(F32)

    def edges(slot):
        col = slot * SLAB
        next_col = col + SLAB if slot % 2 == 0 else ZCOL + (slot // 2) * OWN

        def group(g, acc):
            rows = pl.ds(pl.multiple_of(g * 16, 16), 16)

            def load(ref, start):
                return ref[rows, pl.ds(start, NY)].astype(F32)

            def diffs(ref, r, here):
                ahead = load(ref, col + (r + 1) * NY)
                side = pltpu.roll(here, NY - 1, 1)
                below = load(ref, next_col + r * NY)
                return ahead, ahead - here, side - here, below - here

            new = list(acc)
            u = load(field, col)
            v = [load(psi.at[k], col) for k in range(2)]
            for r in range(ROWS):
                u_next, ux, uy, uz = diffs(field, r, u)
                uy = uy * lane_keep
                if r == ROWS - 1:
                    ux = ux * row_keep
                if slot == 3:
                    uz = uz * depth_keep
                for k in range(2):
                    v_next, vx, vy, vz = diffs(psi.at[k], r, v[k])
                    term = ux * vx + uy * vy + uz * vz
                    new[k * ROWS + r] = new[k * ROWS + r] + term[:8] + term[8:]
                    v[k] = v_next
                u = u_next
            return tuple(new)

        acc = lax.fori_loop(0, ELECTRODES // 16, group, tuple(jnp.zeros((8, NY), F32) for _ in range(2 * ROWS)))
        for k in range(2):
            for r in range(ROWS):
                sens[slot // 2, k, slot % 2, r:r + 1, :] = jnp.sum(acc[k * ROWS + r], axis=0, keepdims=True)

    for slot in range(4):
        edges(slot)

    swap = pltpu.make_async_remote_copy(
        src_ref=sens.at[1 - xl], dst_ref=other, send_sem=ps_sem.at[0], recv_sem=pr_sem.at[0],
        device_id=device_of(xh * 2 + 1 - xl, y, z, c), device_id_type=MESH)
    swap.start()
    mine[...] = sens[xl]
    swap.wait()
    first = jnp.where(xl == 0, mine[...], other[...])
    second = jnp.where(xl == 0, other[...], mine[...])
    full = jnp.concatenate([first, second], axis=2)
    gradient = -(cond[...] * inside[...].astype(F32))[None] * full
    grad_out[...] = gradient
    depth0 = (s * 2).astype(F32)
    weight0 = 1.0 + 2.0 * depth0 / 32.0
    weight1 = 1.0 + 2.0 * (depth0 + 1.0) / 32.0
    run0 = weight0 * gradient[:, 0] * gradient[:, 0]
    run1 = run0 + weight1 * gradient[:, 1] * gradient[:, 1]
    totals[16] = run1

    def total_copy(i):
        return pltpu.make_async_remote_copy(
            src_ref=totals.at[16], dst_ref=totals.at[s], send_sem=ts_sem.at[i], recv_sem=tr_sem.at[s],
            device_id=(e, i), device_id_type=MESH)

    def total_arrival(i):
        return pltpu.make_async_remote_copy(
            src_ref=totals.at[16], dst_ref=totals.at[i], send_sem=ts_sem.at[i], recv_sem=tr_sem.at[i],
            device_id=(e, i), device_id_type=MESH)

    lax.fori_loop(s + 1, 16, lambda i, _: (total_copy(i).start(), 0)[1], 0)

    def add_total(i, before):
        total_arrival(i).wait_recv()
        return before + totals[i]
    prefix = lax.fori_loop(0, s, add_total, jnp.zeros((2, 8, NY), F32))
    scaled_out[:, 0] = gradient[:, 0] / jnp.sqrt(1.0 + (prefix + run0) / (depth0 + 1.0))
    scaled_out[:, 1] = gradient[:, 1] / jnp.sqrt(1.0 + (prefix + run1) / (depth0 + 2.0))

    lax.fori_loop(s + 1, 16, lambda i, _: (total_copy(i).wait_send(), 0)[1], 0)
    for p in range(2):
        for i in range(n_off):
            slab_copy(p, i).wait_send()
    for j in range(2):
        halo_copy(j).wait_send()
    for d in (1, 3, 2):
        w_copy(d).wait_send()
    for d in range(4):
        w_across(d).wait_send()


def per_device(potentials, measurements, residuals, conductivity, inside):
    vmem = pl.BlockSpec(memory_space=pltpu.VMEM)
    dma = pltpu.SemaphoreType.DMA
    shape = jax.ShapeDtypeStruct((2, 2, 8, NY), F32)
    n_off = len(OFFSETS)
    gradient, scaled = pl.pallas_call(
        kernel_body,
        out_shape=(shape, shape),
        in_specs=[pl.BlockSpec(memory_space=pl.ANY), vmem, vmem, vmem, vmem],
        out_specs=(vmem, vmem),
        scratch_shapes=[
            pltpu.VMEM((2, 128, 8192), F32),
            pltpu.VMEM((2, 128, 8192 + NY), BF),
            pltpu.VMEM((ELECTRODES, 4 * SLAB + 2 * OWN), BF),
            pltpu.VMEM((2, ELECTRODES, ELECTRODES), BF),
            pltpu.VMEM((2, 256, 512), F32),
            pltpu.VMEM((2, ELECTRODES, 4 * SLAB + 2 * OWN), BF),
            pltpu.VMEM((2, 2, 2, ROWS, NY), F32),
            pltpu.VMEM((2, 2, ROWS, NY), F32),
            pltpu.VMEM((2, 2, ROWS, NY), F32),
            pltpu.VMEM((17, 2, 8, NY), F32),
            dma((2, 4)), dma((2,)), dma((2, n_off)), dma((2, n_off)), dma((2,)), dma((2,)),
            dma((4,)), dma((4,)), dma((4,)), dma((4,)), dma((1,)), dma((1,)), dma((16,)), dma((16,)),
        ],
        compiler_params=pltpu.CompilerParams(collective_id=0, has_side_effects=True, vmem_limit_bytes=60 << 20),
        name="misfit_gradient",
    )(potentials, measurements.T, residuals, conductivity.reshape(2, 8, NY), inside.reshape(2, 8, NY))
    return gradient.reshape(2, 2, 1024), scaled.reshape(2, 2, 1024)


def solution(mesh):
    return jax.shard_map(
        per_device,
        mesh=mesh,
        in_specs=(P("space", "elec", None), P(), P(), P("space", "elec"), P("space", "elec")),
        out_specs=(P(None, "space", "elec"), P(None, "space", "elec")),
        check_vma=False,
    )
```

profile of v0, /device:TPU:33, one launch (start us, length us, event | category | flops | bytes accessed | tf_op | source)
XLA Modules:
  0.0 123.2 jit_solution(125518614854864014)
XLA Ops:
  0.6 1.3 %copy.12 = f32[1,2,8,128]{3,2,1,0:T(8,128)} copy(f32[1,2,8,128]{3,1,2,0:T(2,128)} %bitcast.16) | data formatting | bytes 16384
  1.9 1.3 %copy.11 = s32[1,2,8,128]{3,2,1,0:T(8,128)} copy(s32[1,2,8,128]{3,1,2,0:T(2,128)} %bitcast.17) | data formatting | bytes 16384
  3.2 117.3 %misfit_gradient.1 = (f32[2,2,8,128]{3,2,1,0:T(8,128)}, f32[2,2,8,128]{3,2,1,0:T(8,128)}) custom-call(f32[2,128,8192]{2,1,0:T(8,128)} %pot.1, s32[4,16384]{1,0:T(4,128)} %bitcast.13, f32[2,16384]{1,0:T(2,128)} %resid.1, f32[2,8,128]{2,1,0:T(8,128)} %bitcast.14, s32[2,8,128]{2,1,0:T(8,128)} %bitcast.15), custom_call_target="tpu_custom_call" | custom-call | tf_op jit(solution)/shard_map/misfit_gradient/pallas_call | solution.py:280
  120.6 1.3 %reshape.18 = f32[2,2,1024]{2,1,0:T(2,128)} reshape(f32[2,2,8,128]{3,2,1,0:T(8,128)} %get-tuple-element.4) | data formatting | bytes 32768 | tf_op jit(solution)/shard_map/reshape | solution.py:302
  121.9 1.3 %reshape.19 = f32[2,2,1024]{2,1,0:T(2,128)} reshape(f32[2,2,8,128]{3,2,1,0:T(8,128)} %get-tuple-element.5) | data formatting | bytes 32768 | tf_op jit(solution)/shard_map/reshape | solution.py:302
where the time goes:
time: 124 us; the launch traced here: 123 us
  Pallas kernels  117 us (94%)
  local copies, waits for them, and re-layouts  5.26 us (4%)
    pallas_call x1, Pallas kernels, per_device(): pl.pallas_call(kernel_body, out_shape=(shape, shape), in_specs=[pl.BlockS...  117 us
    reshape x2, local copies, waits for them, and re-layouts, per_device(): return (gradient.reshape(2, 2, 1024), scaled.reshape(2, 2, 1024))  2.67 us
    unnamed x2, local copies, waits for them, and re-layouts  2.59 us

commit v1 on v0

--- a/solution.py
+++ b/solution.py
@@ -17,6 +17,8 @@
 F32 = jnp.float32
 OFFSETS = [(2, 2), (1, 0), (0, 3), (2, 1), (3, 0), (0, 1), (1, 2), (3, 3), (2, 0), (0, 2), (1, 1), (3, 2), (2, 3), (1, 3), (3, 1)]
 QUAD_CHUNK = 1024
+GROUP = 256
+ADJ_ROWS = 1024
 ZCOL = 4 * SLAB
 
 
@@ -25,9 +27,10 @@
 
 
 def kernel_body(pot, quads, resid, cond, inside, grad_out, scaled_out,
-                stage, send, field, weights, wacc, psi, sens, mine, other, totals,
+                stage, send, field, weights, sym, wacc, adj, cond_t, q_own, q_ahead, cross, q_row, q_row_in, q_depth_in,
+                sens, other, totals,
                 stage_sem, own_sem, out_sem, in_sem, zs_sem, zr_sem, ws_sem, wr_sem, ds_sem, dr_sem,
-                ps_sem, pr_sem, ts_sem, tr_sem):
+                ps_sem, pr_sem, ts_sem, tr_sem, qs_sem, qr_sem):
     e = lax.axis_index("elec")
     s = lax.axis_index("space")
     y = lax.rem(e, 4)
@@ -55,15 +58,18 @@
     for i in range(1, 16):
         pl.semaphore_signal(bar, inc=1, device_id=(e, lax.rem(s + i, 16)), device_id_type=MESH)
 
-    def slab_copy(p, i):
+    pieces = [(0, 0, 5), (1, 0, 3), (1, 3, 2)]
+
+    def slab_copy(m, i):
+        p, row0, rows = pieces[m]
         dx, dy = OFFSETS[i]
         tx = lax.rem(x + dx, 4)
         ty = lax.rem(y + dy, 4)
         block = (lax.div(tx, 2) * 4 + ty) * 2 + lax.rem(tx, 2)
         return pltpu.make_async_remote_copy(
-            src_ref=send.at[p, :, pl.ds(pl.multiple_of(block * OWN, OWN), SLAB)],
-            dst_ref=field.at[pl.ds(pl.multiple_of(e * 128, 128), 128), pl.ds(pl.multiple_of((xl * 2 + p) * SLAB, 128), SLAB)],
-            send_sem=out_sem.at[p, i], recv_sem=in_sem.at[p, i],
+            src_ref=send.at[p, :, pl.ds(pl.multiple_of(block * OWN + row0 * NY, 128), rows * NY)],
+            dst_ref=field.at[pl.ds(pl.multiple_of(e * 128, 128), 128), pl.ds(pl.multiple_of((xl * 2 + p) * SLAB + row0 * NY, 128), rows * NY)],
+            send_sem=out_sem.at[m, i], recv_sem=in_sem.at[m, i],
             device_id=device_of(tx, ty, z, c), device_id_type=MESH)
 
     row_block = e * 2 + xl
@@ -87,8 +93,9 @@
             lax.fori_loop(0, 8, cast, 0)
         if p == 0:
             pl.semaphore_wait(bar, n_off + 15)
-        for i in range(n_off):
-            slab_copy(p, i).start()
+        for m in ((0,), (1, 2))[p]:
+            for i in range(n_off):
+                slab_copy(m, i).start()
         own_copy(p).start()
 
     quarter_f = 256
@@ -155,91 +162,145 @@
     for d in (0, 1, 3, 2):
         w_across(d).wait_recv()
 
-    def adjoint(col, width):
+    def symmetrize(i, _):
+        k = lax.div(i, 16)
+        rows = pl.ds(pl.multiple_of(lax.rem(lax.div(i, 4), 4) * 256, 256), 256)
+        cols = pl.ds(pl.multiple_of(lax.rem(i, 4) * 256, 256), 256)
+        sym[k, rows, cols] = (weights[k, rows, cols].astype(F32) + weights[k, cols, rows].astype(F32).T).astype(BF)
+        return 0
+    lax.fori_loop(0, 32, symmetrize, 0)
+
+    lane_keep = (lax.broadcasted_iota(jnp.int32, (8, NY), 1) < NY - 1).astype(F32)
+    row_keep = (row_block < 15).astype(F32)
+    depth_keep = jnp.logical_or(c == 0, z < 3).astype(F32)
+
+    def work(slot, r0):
+        col = slot * SLAB
+        odd = slot % 2 == 1
+        cols = pl.ds(col + r0 * NY, 2 * NY)
+
         def block(i, _):
-            k = lax.div(i, 4)
-            rows = pl.ds(pl.multiple_of(lax.rem(i, 4) * 256, 256), 256)
-            cols = pl.ds(col, width)
-            psi[k, rows, cols] = jnp.dot(weights[k, rows, :], field[:, cols], preferred_element_type=F32).astype(BF)
+            k = lax.div(i, 1024 // ADJ_ROWS)
+            rows = pl.ds(pl.multiple_of(lax.rem(i, 1024 // ADJ_ROWS) * ADJ_ROWS, ADJ_ROWS), ADJ_ROWS)
+            adj[k, rows, :] = jnp.dot(sym[k, rows, :], field[:, cols], preferred_element_type=F32)
             return 0
-        lax.fori_loop(0, 8, block, 0)
-
-    adjoint(0, SLAB)
-    adjoint(2 * SLAB, SLAB)
-
+        lax.fori_loop(0, 2048 // ADJ_ROWS, block, 0)
+
+        def group(g, acc):
+            rows = pl.ds(pl.multiple_of(g * GROUP, GROUP), GROUP)
+
+            def load(start):
+                return field[rows, pl.ds(start, NY)].astype(F32)
+
+            new = list(acc)
+            n = 0
+            u = load(col + r0 * NY)
+            for r in (r0, r0 + 1):
+                ahead = load(col + (r + 1) * NY)
+                near = (ahead * row_keep if r == ROWS - 1 else ahead) + pltpu.roll(u, NY - 1, 1) * lane_keep[:1]
+                if odd:
+                    below = load(ZCOL + (slot // 2) * OWN + r * NY)
+                    near = near + (below * depth_keep if slot == 3 else below)
+                    above = load(col - SLAB + r * NY)
+                for k in range(2):
+                    v = adj[k, rows, pl.ds((r - r0) * NY, NY)]
+                    for other_u in ((u, near, above) if odd else (u, near)):
+                        t = other_u * v
+                        new[n] = new[n] + jnp.sum(t.reshape(GROUP // 8, 8, NY), axis=0)
+                        n += 1
+                u = ahead
+            return tuple(new)
+
+        per = 3 if odd else 2
+        acc = lax.fori_loop(0, ELECTRODES // GROUP, group, tuple(jnp.zeros((8, NY), F32) for _ in range(4 * per)))
+        n = 0
+        for r in (r0, r0 + 1):
+            for k in range(2):
+                row = k * ROWS + r
+                total = [jnp.sum(acc[n + t], axis=0, keepdims=True) for t in range(per)]
+                n += per
+                q = 0.5 * total[0]
+                q_own[slot, row:row + 1, :] = q
+                if r > 0:
+                    q_ahead[slot, row - 1:row, :] = q
+                else:
+                    q_row[slot * 2 + k:slot * 2 + k + 1, :] = q
+                cross[slot, row:row + 1, :] = total[1]
+                if odd:
+                    cross[slot - 1, row:row + 1, :] += total[2]
+
+    def q_depth_copy(j):
+        slot = jnp.where(c == 0, 2 - 2 * j, 2 * j)
+        if j == 0:
+            target = device_of(x, y, z, 1 - c)
+        else:
+            target = device_of(x, y, jnp.where(c == 0, lax.rem(z + 3, 4), z), 1 - c)
+        return pltpu.make_async_remote_copy(
+            src_ref=q_own.at[slot], dst_ref=q_depth_in.at[j], send_sem=qs_sem.at[j], recv_sem=qr_sem.at[j],
+            device_id=target, device_id_type=MESH)
+
+    def q_row_copy():
+        before = lax.rem(row_block + 15, 16)
+        be = lax.div(before, 2)
+        return pltpu.make_async_remote_copy(
+            src_ref=q_row, dst_ref=q_row_in, send_sem=qs_sem.at[2], recv_sem=qr_sem.at[2],
+            device_id=(be, z * 4 + lax.rem(before, 2) * 2 + c), device_id_type=MESH)
+
+    for slot in (0, 2):
+        for r0 in (0, 2):
+            work(slot, r0)
+    for j in (0, 1):
+        q_depth_copy(j).start()
     for j in range(2):
         halo_copy(j).wait_recv()
-        adjoint(ZCOL + j * OWN, OWN)
-
     for i in range(n_off):
         slab_copy(1, i).wait_recv()
     own_copy(1).wait()
-    adjoint(SLAB, SLAB)
-    adjoint(3 * SLAB, SLAB)
-
-    lane_keep = (lax.broadcasted_iota(jnp.int32, (16, NY), 1) < NY - 1).astype(F32)
-    row_keep = (row_block < 15).astype(F32)
-    depth_keep = jnp.logical_or(c == 0, z < 3).astype(F32)
-
-    def edges(slot):
-        col = slot * SLAB
-        next_col = col + SLAB if slot % 2 == 0 else ZCOL + (slot // 2) * OWN
-
-        def group(g, acc):
-            rows = pl.ds(pl.multiple_of(g * 16, 16), 16)
-
-            def load(ref, start):
-                return ref[rows, pl.ds(start, NY)].astype(F32)
-
-            def diffs(ref, r, here):
-                ahead = load(ref, col + (r + 1) * NY)
-                side = pltpu.roll(here, NY - 1, 1)
-                below = load(ref, next_col + r * NY)
-                return ahead, ahead - here, side - here, below - here
-
-            new = list(acc)
-            u = load(field, col)
-            v = [load(psi.at[k], col) for k in range(2)]
-            for r in range(ROWS):
-                u_next, ux, uy, uz = diffs(field, r, u)
-                uy = uy * lane_keep
-                if r == ROWS - 1:
-                    ux = ux * row_keep
-                if slot == 3:
-                    uz = uz * depth_keep
-                for k in range(2):
-                    v_next, vx, vy, vz = diffs(psi.at[k], r, v[k])
-                    term = ux * vx + uy * vy + uz * vz
-                    new[k * ROWS + r] = new[k * ROWS + r] + term[:8] + term[8:]
-                    v[k] = v_next
-                u = u_next
-            return tuple(new)
-
-        acc = lax.fori_loop(0, ELECTRODES // 16, group, tuple(jnp.zeros((8, NY), F32) for _ in range(2 * ROWS)))
+    for slot in (1, 3):
+        work(slot, 0)
+    q_row_copy().start()
+    for i in range(n_off):
+        slab_copy(2, i).wait_recv()
+    for slot in (1, 3):
+        work(slot, 2)
+    for j in range(2):
+        q_depth_copy(j).wait_recv()
+    q_row_copy().wait_recv()
+
+    edge_lane = lane_keep
+    sub_row = lax.rem(lax.broadcasted_iota(jnp.int32, (8, NY), 0), ROWS)
+    x_valid = jnp.where(sub_row == ROWS - 1, row_keep, 1.0)
+    for slot in range(4):
         for k in range(2):
-            for r in range(ROWS):
-                sens[slot // 2, k, slot % 2, r:r + 1, :] = jnp.sum(acc[k * ROWS + r], axis=0, keepdims=True)
-
-    for slot in range(4):
-        edges(slot)
+            row = k * ROWS + ROWS - 1
+            q_ahead[slot, row:row + 1, :] = q_row_in[slot * 2 + k:slot * 2 + k + 1, :] * row_keep
+        z_valid = depth_keep if slot == 3 else 1.0
+        q = q_own[slot]
+        q_below = q_own[slot + 1] if slot % 2 == 0 else q_depth_in[slot // 2] * z_valid
+        sens[slot] = (x_valid + edge_lane + z_valid) * q + q_ahead[slot] + pltpu.roll(q, NY - 1, 1) * edge_lane + q_below - cross[slot]
 
     swap = pltpu.make_async_remote_copy(
-        src_ref=sens.at[1 - xl], dst_ref=other, send_sem=ps_sem.at[0], recv_sem=pr_sem.at[0],
+        src_ref=sens.at[pl.ds(2 * (1 - xl), 2)], dst_ref=other, send_sem=ps_sem.at[0], recv_sem=pr_sem.at[0],
         device_id=device_of(xh * 2 + 1 - xl, y, z, c), device_id_type=MESH)
     swap.start()
-    mine[...] = sens[xl]
+    rate = -(cond[...] * inside[...].astype(F32))
+    for p in range(2):
+        for r in range(8):
+            cond_t[p, r:r + 1, :] = rate[p:p + 1, r * NY:(r + 1) * NY]
+    mine = sens[pl.ds(2 * xl, 2)]
     swap.wait()
-    first = jnp.where(xl == 0, mine[...], other[...])
-    second = jnp.where(xl == 0, other[...], mine[...])
-    full = jnp.concatenate([first, second], axis=2)
-    gradient = -(cond[...] * inside[...].astype(F32))[None] * full
-    grad_out[...] = gradient
+    theirs = other[...]
+    first = jnp.where(xl == 0, mine, theirs)
+    second = jnp.where(xl == 0, theirs, mine)
+    gradient = [[cond_t[p] * jnp.concatenate([first[p, k * ROWS:(k + 1) * ROWS], second[p, k * ROWS:(k + 1) * ROWS]], axis=0)
+                 for p in range(2)] for k in range(2)]
     depth0 = (s * 2).astype(F32)
     weight0 = 1.0 + 2.0 * depth0 / 32.0
     weight1 = 1.0 + 2.0 * (depth0 + 1.0) / 32.0
-    run0 = weight0 * gradient[:, 0] * gradient[:, 0]
-    run1 = run0 + weight1 * gradient[:, 1] * gradient[:, 1]
-    totals[16] = run1
+    run0 = [weight0 * gradient[k][0] * gradient[k][0] for k in range(2)]
+    run1 = [run0[k] + weight1 * gradient[k][1] * gradient[k][1] for k in range(2)]
+    for k in range(2):
+        totals[16, k] = run1[k]
 
     def total_copy(i):
         return pltpu.make_async_remote_copy(
@@ -257,13 +318,21 @@
         total_arrival(i).wait_recv()
         return before + totals[i]
     prefix = lax.fori_loop(0, s, add_total, jnp.zeros((2, 8, NY), F32))
-    scaled_out[:, 0] = gradient[:, 0] / jnp.sqrt(1.0 + (prefix + run0) / (depth0 + 1.0))
-    scaled_out[:, 1] = gradient[:, 1] / jnp.sqrt(1.0 + (prefix + run1) / (depth0 + 2.0))
+    for k in range(2):
+        for p, run in ((0, run0[k]), (1, run1[k])):
+            g = gradient[k][p]
+            scaled = g / jnp.sqrt(1.0 + (prefix[k] + run) / (depth0 + (p + 1.0)))
+            for r in range(8):
+                grad_out[k, p:p + 1, r * NY:(r + 1) * NY] = g[r:r + 1]
+                scaled_out[k, p:p + 1, r * NY:(r + 1) * NY] = scaled[r:r + 1]
 
     lax.fori_loop(s + 1, 16, lambda i, _: (total_copy(i).wait_send(), 0)[1], 0)
-    for p in range(2):
+    for m in range(3):
         for i in range(n_off):
-            slab_copy(p, i).wait_send()
+            slab_copy(m, i).wait_send()
+    for j in range(2):
+        q_depth_copy(j).wait_send()
+    q_row_copy().wait_send()
     for j in range(2):
         halo_copy(j).wait_send()
     for d in (1, 3, 2):
@@ -275,9 +344,10 @@
 def per_device(potentials, measurements, residuals, conductivity, inside):
     vmem = pl.BlockSpec(memory_space=pltpu.VMEM)
     dma = pltpu.SemaphoreType.DMA
-    shape = jax.ShapeDtypeStruct((2, 2, 8, NY), F32)
+    shape = jax.ShapeDtypeStruct((2, 2, 1024), F32)
     n_off = len(OFFSETS)
-    gradient, scaled = pl.pallas_call(
+    tile = (8, NY)
+    return pl.pallas_call(
         kernel_body,
         out_shape=(shape, shape),
         in_specs=[pl.BlockSpec(memory_space=pl.ANY), vmem, vmem, vmem, vmem],
@@ -287,19 +357,25 @@
             pltpu.VMEM((2, 128, 8192 + NY), BF),
             pltpu.VMEM((ELECTRODES, 4 * SLAB + 2 * OWN), BF),
             pltpu.VMEM((2, ELECTRODES, ELECTRODES), BF),
+            pltpu.VMEM((2, ELECTRODES, ELECTRODES), BF),
             pltpu.VMEM((2, 256, 512), F32),
-            pltpu.VMEM((2, ELECTRODES, 4 * SLAB + 2 * OWN), BF),
-            pltpu.VMEM((2, 2, 2, ROWS, NY), F32),
-            pltpu.VMEM((2, 2, ROWS, NY), F32),
-            pltpu.VMEM((2, 2, ROWS, NY), F32),
-            pltpu.VMEM((17, 2, 8, NY), F32),
-            dma((2, 4)), dma((2,)), dma((2, n_off)), dma((2, n_off)), dma((2,)), dma((2,)),
-            dma((4,)), dma((4,)), dma((4,)), dma((4,)), dma((1,)), dma((1,)), dma((16,)), dma((16,)),
+            pltpu.VMEM((2, ELECTRODES, 2 * NY), F32),
+            pltpu.VMEM((2,) + tile, F32),
+            pltpu.VMEM((4,) + tile, F32),
+            pltpu.VMEM((4,) + tile, F32),
+            pltpu.VMEM((4,) + tile, F32),
+            pltpu.VMEM(tile, F32),
+            pltpu.VMEM(tile, F32),
+            pltpu.VMEM((2,) + tile, F32),
+            pltpu.VMEM((4,) + tile, F32),
+            pltpu.VMEM((2,) + tile, F32),
+            pltpu.VMEM((17, 2) + tile, F32),
+            dma((2, 4)), dma((2,)), dma((3, n_off)), dma((3, n_off)), dma((2,)), dma((2,)),
+            dma((4,)), dma((4,)), dma((4,)), dma((4,)), dma((1,)), dma((1,)), dma((16,)), dma((16,)), dma((3,)), dma((3,)),
         ],
         compiler_params=pltpu.CompilerParams(collective_id=0, has_side_effects=True, vmem_limit_bytes=60 << 20),
         name="misfit_gradient",
-    )(potentials, measurements.T, residuals, conductivity.reshape(2, 8, NY), inside.reshape(2, 8, NY))
-    return gradient.reshape(2, 2, 1024), scaled.reshape(2, 2, 1024)
+    )(potentials, measurements.T, residuals, conductivity, inside)
 
 
 def solution(mesh):

time: 124 us -> 92.7 us (0.75)
  Pallas kernels: 117 us -> 89.1 us
  local copies, waits for them, and re-layouts: 5.26 us -> 2.65 us
    pallas_call x1, Pallas kernels: 117 us -> 89.1 us  [per_device(): pl.pallas_call(kernel_body, out_shape=(shape, shape), in_specs=[pl.BlockS...]
    reshape x2 -> x0, local copies, waits for them, and re-layouts: 2.67 us -> none  [per_device(): return (gradient.reshape(2, 2, 1024), scaled.reshape(2, 2, 1024))]
where the time goes in v1:
time: 92.7 us; the launch traced here: 92.4 us
  Pallas kernels  89.1 us (96%)
  local copies, waits for them, and re-layouts  2.65 us (3%)
    pallas_call x1, Pallas kernels, per_device(): pl.pallas_call(kernel_body, out_shape=(shape, shape), in_specs=[pl.BlockS...  89.1 us
    unnamed x2, local copies, waits for them, and re-layouts  2.65 us

profile of v1, /device:TPU:33, one launch (start us, length us, event | category | flops | bytes accessed | tf_op | source)
XLA Modules:
  0.0 92.4 jit_solution(7087867813271970869)
XLA Ops:
  0.6 89.1 %misfit_gradient.1 = (f32[2,2,1024]{2,1,0:T(2,128)}, f32[2,2,1024]{2,1,0:T(2,128)}) custom-call(f32[2,128,8192]{2,1,0:T(8,128)} %pot.1, s32[4,16384]{1,0:T(4,128)} %bitcast.1, f32[2,16384]{1,0:T(2,128)} %resid.1, f32[2,1024]{1,0:T(2,128)} %cond.1, s32[2,1024]{1,0:T(2,128)} %inside.1), custom_call_target="tpu_custom_call" | custom-call | tf_op jit(solution)/shard_map/misfit_gradient/pallas_call | solution.py:350
  89.8 1.3 %copy.9 = f32[2,2,1024]{2,1,0:T(2,128)} copy(f32[2,2,1024]{2,1,0:T(2,128)} %get-tuple-element.4) | data formatting | bytes 32768
  91.1 1.3 %copy.10 = f32[2,2,1024]{2,1,0:T(2,128)} copy(f32[2,2,1024]{2,1,0:T(2,128)} %get-tuple-element.5) | data formatting | bytes 32768

commit v2 on v1

v2 whole, which is shorter than its diff:
```python
import functools

import jax
import jax.numpy as jnp
from jax import lax
from jax.experimental import pallas as pl
from jax.experimental.pallas import tpu as pltpu
from jax.sharding import PartitionSpec as P

ELECTRODES = 1024
NY = 128
ROWS = 4
SLAB = (ROWS + 1) * NY
OWN = ROWS * NY
MESH = pl.DeviceIdType.MESH
BF = jnp.bfloat16
F32 = jnp.float32
QUAD_CHUNK = 2048
XROWS = 4 * ROWS + 1
GROUP = 256
ADJ_ROWS = 1024
ZCOL = 4 * SLAB


def device_of(x, y, z, c):
    return (lax.div(x, 2) * 4 + y, z * 4 + lax.rem(x, 2) * 2 + c)


def kernel_body(pot, quads, resid, cond, inside, grad_out, scaled_out,
                stage, send, mid, field, weights, sym, wacc, adj, cond_t, q_own, q_ahead, cross, q_row, q_row_in, q_depth_in,
                sens, other, totals,
                stage_sem, loc_sem, xs_sem, xr_sem, ys_sem, yr_sem, zs_sem, zr_sem, ws_sem, wr_sem, ds_sem, dr_sem,
                ps_sem, pr_sem, ts_sem, tr_sem, qs_sem, qr_sem):
    e = lax.axis_index("elec")
    s = lax.axis_index("space")
    y = lax.rem(e, 4)
    xh = lax.div(e, 4)
    c = lax.rem(s, 2)
    xl = lax.rem(lax.div(s, 2), 2)
    z = lax.div(s, 4)
    x = xh * 2 + xl
    row_block = x * 4 + y

    cells = pot.shape[2]
    quarter = cells // 4

    def stage_copy(p, q):
        cols = pl.ds(q * quarter, quarter)
        return pltpu.make_async_copy(pot.at[p, :, cols], stage.at[p, :, cols], stage_sem.at[p, q])

    for p in range(2):
        for q in range(4):
            stage_copy(p, q).start()

    def owner(j):
        return device_of(lax.div(x, 2) * 2 + j, 2 * lax.rem(x, 2) + lax.div(y, 2), z, c)

    def owner_is_me(j):
        return jnp.logical_and(xl == j, y == 2 * xl + lax.div(y, 2))

    def holder(h):
        return device_of(2 * xh + lax.div(y, 2), 2 * lax.rem(y, 2) + h, z, c)

    def holder_is_me(h):
        return jnp.logical_and(x == 2 * xh + lax.div(y, 2), y == 2 * lax.rem(y, 2) + h)

    def row_device(b):
        return device_of(lax.div(b, 4), lax.rem(b, 4), z, c)

    bar = pltpu.get_barrier_semaphore()

    def greet(device):
        pl.semaphore_signal(bar, inc=1, device_id=device, device_id_type=MESH)

    for d in range(1, 4):
        greet(device_of(lax.rem(x + d, 4), y, z, c))
        greet(device_of(x, lax.rem(y + d, 4), z, c))
    greet(row_device(lax.rem(row_block + 1, 16)))
    for i in range(1, 16):
        greet((e, lax.rem(s + i, 16)))
    targets = 0
    for j in range(2):
        @pl.when(jnp.logical_not(holder_is_me(j)))
        def _():
            greet(holder(j))
        targets = targets + jnp.where(owner_is_me(j), 0, 1)

    def x_parts():
        return ((0, 64), (64, 64))

    def x_copy(p, d, h):
        tx = lax.rem(x + 4 - d, 4)
        rows = pl.ds(*x_parts()[h])
        return pltpu.make_async_remote_copy(
            src_ref=send.at[p, rows, pl.ds(pl.multiple_of(tx * (4 * OWN), 128), XROWS * NY)], dst_ref=mid.at[p, d - 1, rows],
            send_sem=xs_sem.at[p, d, h], recv_sem=xr_sem.at[p, d, h],
            device_id=device_of(tx, y, z, c), device_id_type=MESH)

    def pieces(p, d):
        if d == 0:
            return ((0, 0, 5),)
        if p == 1 and d == 2:
            return ((0, 0, 5), (1, 0, 3), (1, 3, 2))
        return ((0, 0, 5), (1, 0, 5))

    def slab(p, d, ty, first_e, count, row0, rows):
        xs = lax.rem(x + d, 4)
        es = pl.ds(first_e, count)
        if d == 0:
            src = send.at[p, es, pl.ds(pl.multiple_of((x * 4 + ty) * OWN + row0 * NY, 128), rows * NY)]
        else:
            src = mid.at[p, d - 1, es, pl.ds(pl.multiple_of(ty * OWN + row0 * NY, 128), rows * NY)]
        dst = field.at[pl.ds(pl.multiple_of(lax.div(xs, 2) * 512 + y * 128 + first_e, 64), count),
                       pl.ds(pl.multiple_of((lax.rem(xs, 2) * 2 + p) * SLAB + row0 * NY, 128), rows * NY)]
        return src, dst

    def y_copy(p, d, m, dy):
        ty = lax.rem(y + dy, 4)
        h, row0, rows = pieces(p, d)[m]
        src, dst = slab(p, d, ty, *(x_parts()[h] if d > 0 else (0, 128)), row0, rows)
        return pltpu.make_async_remote_copy(
            src_ref=src, dst_ref=dst, send_sem=ys_sem.at[p, d, m, dy], recv_sem=yr_sem.at[p, d, m, dy],
            device_id=device_of(x, ty, z, c), device_id_type=MESH)

    def local_copy(p, d):
        return pltpu.make_async_copy(*slab(p, d, y, 0, 128, 0, 5), loc_sem.at[p, d])

    def y_start(p, d, h=0):
        for m, piece in enumerate(pieces(p, d)):
            if piece[0] == h:
                for dy in (1, 3, 2):
                    y_copy(p, d, m, dy).start()
        if d == 0 or h == len(x_parts()) - 1:
            local_copy(p, d).start()

    def y_wait(p, d, chosen=None):
        for m in range(len(pieces(p, d))) if chosen is None else chosen:
            for dy in (1, 3, 2):
                y_copy(p, d, m, dy).wait_recv()
        if chosen is None or 0 in chosen:
            local_copy(p, d).wait()

    def pass_on(p, d, h=0):
        x_copy(p, d, h).wait_recv()
        y_start(p, d, h)

    for p in range(2):
        send[p, :, pl.ds(cells, NY)] = jnp.zeros((128, NY), BF)
        for q in range(4):
            stage_copy(p, q).wait()

            def cast(i, _):
                rows = pl.ds(pl.multiple_of(i * 16, 16), 16)
                cols = pl.ds(q * quarter, quarter)
                send[p, rows, cols] = stage[p, rows, cols].astype(BF)
                return 0
            lax.fori_loop(0, 8, cast, 0)
        if p == 0:
            pl.semaphore_wait(bar, 22 + targets)
        for d in (1, 3, 2):
            for h in range(len(x_parts())):
                x_copy(p, d, h).start()
        y_start(p, 0)

    quarter_f = 256
    half_e = 512
    def one_hot(plus, minus, base, count):
        parts = []
        for b in range(0, count, 256):
            ids = lax.broadcasted_iota(jnp.int32, (256, QUAD_CHUNK), 0).astype(F32).astype(BF)
            hit = (plus - (base + b)).astype(F32).astype(BF) == ids
            miss = (minus - (base + b)).astype(F32).astype(BF) == ids
            one = jnp.ones((), BF)
            parts.append(jnp.where(hit, one, jnp.where(miss, -one, jnp.zeros((), BF))))
        return parts[0] if len(parts) == 1 else jnp.concatenate(parts, axis=0)

    def add_quads(part, first, last):
        def step(i, _):
            cols = pl.ds(pl.multiple_of(i * QUAD_CHUNK, QUAD_CHUNK), QUAD_CHUNK)
            left = one_hot(quads[2:3, cols], quads[3:4, cols], z * quarter_f, quarter_f)
            right = one_hot(quads[0:1, cols], quads[1:2, cols], c * half_e + part * 256, 256)
            parts = []
            for k in range(2):
                r = resid[k:k + 1, cols]
                hi = r.astype(BF)
                parts += [left * hi, left * (r - hi.astype(F32)).astype(BF)]
            both = lax.dot_general(jnp.concatenate(parts, axis=0), right, (((1,), (1,)), ((), ())), preferred_element_type=F32)
            for k in range(2):
                wacc[part, k] += both[k * 512:k * 512 + 256] + both[k * 512 + 256:k * 512 + 512]
            return 0
        if first == 0:
            wacc[part] = jnp.zeros(wacc.shape[1:], F32)
        lax.fori_loop(first, last, step, 0)

    def block_of(part, zz, cc):
        return weights.at[:, pl.ds(pl.multiple_of(zz * quarter_f, quarter_f), quarter_f),
                          pl.ds(pl.multiple_of(cc * half_e + part * 256, 256), 256)]

    def w_copy(part, d):
        zz = lax.rem(z + 3, 4) if d == 2 else z
        step = 3 if d == 3 else 1
        return pltpu.make_async_remote_copy(
            src_ref=block_of(part, zz, c), dst_ref=block_of(part, zz, c), send_sem=ws_sem.at[part, d], recv_sem=wr_sem.at[part, d],
            device_id=device_of(x, y, lax.rem(z + step, 4), c), device_id_type=MESH)

    def w_across(part, d):
        zz = lax.rem(z + 4 - d, 4)
        return pltpu.make_async_remote_copy(
            src_ref=block_of(part, zz, c), dst_ref=block_of(part, zz, c), send_sem=ds_sem.at[part, d], recv_sem=dr_sem.at[part, d],
            device_id=device_of(x, y, z, 1 - c), device_id_type=MESH)

    def w_share(part):
        weights[:, pl.ds(pl.multiple_of(z * quarter_f, quarter_f), quarter_f),
                pl.ds(pl.multiple_of(c * half_e + part * 256, 256), 256)] = wacc[part].astype(BF)
        w_copy(part, 1).start()
        w_copy(part, 3).start()
        w_across(part, 0).start()

    def w_forward(part):
        w_copy(part, 1).wait_recv()
        w_copy(part, 2).start()
        w_across(part, 1).start()
        w_copy(part, 3).wait_recv()
        w_across(part, 3).start()

    def w_last(part):
        w_copy(part, 2).wait_recv()
        w_across(part, 2).start()

    chunks = quads.shape[1] // QUAD_CHUNK
    def halo_target(pair):
        down = jnp.logical_and(c == 0, pair == 0)
        j = jnp.where(c == 0, 1 - pair, pair)
        return j, device_of(x, y, jnp.where(down, lax.rem(z + 3, 4), z), 1 - c)

    def halo_copy(d):
        xs = lax.rem(x + d, 4)
        pair = lax.rem(xs, 2)
        half = lax.div(xs, 2)
        j, target = halo_target(pair)
        rows = pl.ds(pl.multiple_of(half * 512, 512), 512)
        return pltpu.make_async_remote_copy(
            src_ref=field.at[rows, pl.ds(pl.multiple_of(pair * (2 * SLAB), 128), OWN)],
            dst_ref=field.at[rows, pl.ds(pl.multiple_of(ZCOL + j * OWN, 128), OWN)],
            send_sem=zs_sem.at[d], recv_sem=zr_sem.at[j * 2 + half], device_id=target, device_id_type=MESH)

    def halo_arrival(j, half):
        return pltpu.make_async_remote_copy(
            src_ref=field.at[pl.ds(0, 512), pl.ds(0, OWN)], dst_ref=field.at[pl.ds(half * 512, 512), pl.ds(ZCOL + j * OWN, OWN)],
            send_sem=zs_sem.at[0], recv_sem=zr_sem.at[j * 2 + half], device_id=device_of(x, y, z, 1 - c), device_id_type=MESH)

    def first_planes(d):
        y_wait(0, d)
        halo_copy(d).start()

    def near_on(p, h):
        pass_on(p, 1, h)
        pass_on(p, 3, h)

    eighth = chunks // 8
    add_quads(0, 0, 5 * eighth)
    near_on(0, 0)
    add_quads(0, 5 * eighth, chunks)
    w_share(0)
    add_quads(1, 0, 2 * eighth)
    near_on(0, 1)
    add_quads(1, 2 * eighth, 5 * eighth)
    w_forward(0)
    add_quads(1, 5 * eighth, 7 * eighth)
    pass_on(0, 2, 0)
    add_quads(1, 7 * eighth, chunks)
    w_share(1)
    w_last(0)
    pass_on(0, 2, 1)
    w_forward(1)
    first_planes(0)
    first_planes(1)
    first_planes(3)
    near_on(1, 0)
    w_last(1)
    for part in range(2):
        for d in range(4):
            w_across(part, d).wait_recv()

    def symmetrize(i, _):
        k = lax.div(i, 16)
        rows = pl.ds(pl.multiple_of(lax.rem(lax.div(i, 4), 4) * 256, 256), 256)
        cols = pl.ds(pl.multiple_of(lax.rem(i, 4) * 256, 256), 256)
        sym[k, rows, cols] = (weights[k, rows, cols].astype(F32) + weights[k, cols, rows].T.astype(F32)).astype(BF)
        return 0
    lax.fori_loop(0, 16, symmetrize, 0, unroll=4)
    near_on(1, 1)
    lax.fori_loop(16, 32, symmetrize, 0, unroll=4)
    first_planes(2)

    lane_keep = (lax.broadcasted_iota(jnp.int32, (8, NY), 1) < NY - 1).astype(F32)
    row_keep = (row_block < 15).astype(F32)
    depth_keep = jnp.logical_or(c == 0, z < 3).astype(F32)

    def work(pair, p, r0):
        slot = pair * 2 + p
        col = slot * SLAB
        odd = p == 1
        cols = pl.ds(pl.multiple_of(col + r0 * NY, 128), 2 * NY)
        z_keep = jnp.where(pair == 1, depth_keep, 1.0)

        def block(i, _):
            k = lax.div(i, 1024 // ADJ_ROWS)
            rows = pl.ds(pl.multiple_of(lax.rem(i, 1024 // ADJ_ROWS) * ADJ_ROWS, ADJ_ROWS), ADJ_ROWS)
            adj[k, rows, :] = jnp.dot(sym[k, rows, :], field[:, cols], preferred_element_type=F32)
            return 0
        lax.fori_loop(0, 2048 // ADJ_ROWS, block, 0)

        def group(g, acc):
            rows = pl.ds(pl.multiple_of(g * GROUP, GROUP), GROUP)

            def load(start):
                return field[rows, pl.ds(pl.multiple_of(start, 128), NY)].astype(F32)

            new = list(acc)
            n = 0
            u = load(col + r0 * NY)
            for r in (r0, r0 + 1):
                ahead = load(col + (r + 1) * NY)
                near = (ahead * row_keep if r == ROWS - 1 else ahead) + pltpu.roll(u, NY - 1, 1) * lane_keep[:1]
                if odd:
                    near = near + load(ZCOL + pair * OWN + r * NY) * z_keep
                    above = load(col - SLAB + r * NY)
                for k in range(2):
                    v = adj[k, rows, pl.ds((r - r0) * NY, NY)]
                    for other_u in ((u, near, above) if odd else (u, near)):
                        t = other_u * v
                        new[n] = new[n] + jnp.sum(t.reshape(GROUP // 8, 8, NY), axis=0)
                        n += 1
                u = ahead
            return tuple(new)

        per = 3 if odd else 2
        acc = lax.fori_loop(0, ELECTRODES // GROUP, group, tuple(jnp.zeros((8, NY), F32) for _ in range(4 * per)))
        n = 0
        for r in (r0, r0 + 1):
            for k in range(2):
                row = k * ROWS + r
                total = [jnp.sum(acc[n + t], axis=0, keepdims=True) for t in range(per)]
                n += per
                q = 0.5 * total[0]
                q_own[slot, row:row + 1, :] = q
                if r > 0:
                    q_ahead[slot, row - 1:row, :] = q
                else:
                    q_row[pl.ds(slot * 2 + k, 1), :] = q
                cross[slot, row:row + 1, :] = total[1]
                if odd:
                    cross[slot - 1, row:row + 1, :] += total[2]

    def q_depth_copy(pair):
        j, target = halo_target(pair)
        return pltpu.make_async_remote_copy(
            src_ref=q_own.at[pair * 2], dst_ref=q_depth_in.at[j], send_sem=qs_sem.at[pair], recv_sem=qr_sem.at[j],
            device_id=target, device_id_type=MESH)

    def q_depth_arrival(j):
        return pltpu.make_async_remote_copy(
            src_ref=q_own.at[0], dst_ref=q_depth_in.at[j], send_sem=qs_sem.at[j], recv_sem=qr_sem.at[j],
            device_id=device_of(x, y, z, 1 - c), device_id_type=MESH)

    def q_row_copy():
        return pltpu.make_async_remote_copy(
            src_ref=q_row, dst_ref=q_row_in, send_sem=qs_sem.at[2], recv_sem=qr_sem.at[2],
            device_id=row_device(lax.rem(row_block + 15, 16)), device_id_type=MESH)

    near_pair = 1 - xl
    far_pair = xl
    work(near_pair, 0, 0)
    work(near_pair, 0, 2)
    pass_on(1, 2, 0)
    work(far_pair, 0, 0)
    work(far_pair, 0, 2)
    pass_on(1, 2, 1)
    for j in range(2):
        q_depth_copy(j).start()
    for j in range(2):
        for half in range(2):
            halo_arrival(j, half).wait_recv()
    y_wait(1, 1)
    y_wait(1, 3)
    work(near_pair, 1, 0)
    work(near_pair, 1, 2)
    y_wait(1, 0)
    y_wait(1, 2, (0, 1))
    work(far_pair, 1, 0)
    q_row_copy().start()
    y_wait(1, 2, (2,))
    work(far_pair, 1, 2)
    for j in range(2):
        q_depth_arrival(j).wait_recv()
    q_row_copy().wait_recv()

    edge_lane = lane_keep
    sub_row = lax.rem(lax.broadcasted_iota(jnp.int32, (8, NY), 0), ROWS)
    x_valid = jnp.where(sub_row == ROWS - 1, row_keep, 1.0)
    for slot in range(4):
        for k in range(2):
            row = k * ROWS + ROWS - 1
            q_ahead[slot, row:row + 1, :] = q_row_in[slot * 2 + k:slot * 2 + k + 1, :] * row_keep
        z_valid = depth_keep if slot == 3 else 1.0
        q = q_own[slot]
        q_below = q_own[slot + 1] if slot % 2 == 0 else q_depth_in[slot // 2] * z_valid
        sens[slot] = (x_valid + edge_lane + z_valid) * q + q_ahead[slot] + pltpu.roll(q, NY - 1, 1) * edge_lane + q_below - cross[slot]

    def hand_over(j):
        return pltpu.make_async_remote_copy(
            src_ref=sens.at[pl.ds(2 * j, 2)], dst_ref=other.at[lax.rem(y, 2)], send_sem=ps_sem.at[j], recv_sem=pr_sem.at[lax.rem(y, 2)],
            device_id=owner(j), device_id_type=MESH)

    def hand_over_arrival(h):
        return pltpu.make_async_remote_copy(
            src_ref=sens.at[pl.ds(0, 2)], dst_ref=other.at[h], send_sem=ps_sem.at[h], recv_sem=pr_sem.at[h],
            device_id=holder(h), device_id_type=MESH)

    for j in range(2):
        @pl.when(jnp.logical_not(owner_is_me(j)))
        def _():
            hand_over(j).start()

        @pl.when(owner_is_me(j))
        def _():
            other[lax.rem(y, 2)] = sens[pl.ds(2 * j, 2)]
    rate = -(cond[...] * inside[...].astype(F32))
    for p in range(2):
        for r in range(8):
            cond_t[p, r:r + 1, :] = rate[p:p + 1, r * NY:(r + 1) * NY]
    for h in range(2):
        @pl.when(jnp.logical_not(holder_is_me(h)))
        def _():
            hand_over_arrival(h).wait_recv()
    first = other[0]
    second = other[1]
    gradient = [[cond_t[p] * jnp.concatenate([first[p, k * ROWS:(k + 1) * ROWS], second[p, k * ROWS:(k + 1) * ROWS]], axis=0)
                 for p in range(2)] for k in range(2)]
    depth0 = (s * 2).astype(F32)
    weight0 = 1.0 + 2.0 * depth0 / 32.0
    weight1 = 1.0 + 2.0 * (depth0 + 1.0) / 32.0
    run0 = [weight0 * gradient[k][0] * gradient[k][0] for k in range(2)]
    run1 = [run0[k] + weight1 * gradient[k][1] * gradient[k][1] for k in range(2)]
    for k in range(2):
        totals[16, k] = run1[k]

    def total_copy(i):
        return pltpu.make_async_remote_copy(
            src_ref=totals.at[16], dst_ref=totals.at[s], send_sem=ts_sem.at[i], recv_sem=tr_sem.at[s],
            device_id=(e, i), device_id_type=MESH)

    def total_arrival(i):
        return pltpu.make_async_remote_copy(
            src_ref=totals.at[16], dst_ref=totals.at[i], send_sem=ts_sem.at[i], recv_sem=tr_sem.at[i],
            device_id=(e, i), device_id_type=MESH)

    lax.fori_loop(s + 1, 16, lambda i, _: (total_copy(i).start(), 0)[1], 0)

    def add_total(i, before):
        total_arrival(i).wait_recv()
        return before + totals[i]
    prefix = lax.fori_loop(0, s, add_total, jnp.zeros((2, 8, NY), F32))
    for k in range(2):
        for p, run in ((0, run0[k]), (1, run1[k])):
            g = gradient[k][p]
            scaled = g / jnp.sqrt(1.0 + (prefix[k] + run) / (depth0 + (p + 1.0)))
            for r in range(8):
                grad_out[k, p:p + 1, r * NY:(r + 1) * NY] = g[r:r + 1]
                scaled_out[k, p:p + 1, r * NY:(r + 1) * NY] = scaled[r:r + 1]

    lax.fori_loop(s + 1, 16, lambda i, _: (total_copy(i).wait_send(), 0)[1], 0)
    for p in range(2):
        for d in range(4):
            if d > 0:
                for h in range(len(x_parts())):
                    x_copy(p, d, h).wait_send()
            for m in range(len(pieces(p, d))):
                for dy in (1, 3, 2):
                    y_copy(p, d, m, dy).wait_send()
    for j in range(2):
        q_depth_copy(j).wait_send()

        @pl.when(jnp.logical_not(owner_is_me(j)))
        def _():
            hand_over(j).wait_send()
    q_row_copy().wait_send()
    for d in range(4):
        halo_copy(d).wait_send()
    for part in range(2):
        for d in (1, 3, 2):
            w_copy(part, d).wait_send()
        for d in range(4):
            w_across(part, d).wait_send()


def per_device(potentials, measurements, residuals, conductivity, inside):
    vmem = pl.BlockSpec(memory_space=pltpu.VMEM)
    dma = pltpu.SemaphoreType.DMA
    shape = jax.ShapeDtypeStruct((2, 2, 1024), F32)
    tile = (8, NY)
    results = pl.pallas_call(
        kernel_body,
        out_shape=(shape, shape),
        in_specs=[pl.BlockSpec(memory_space=pl.ANY), vmem, vmem, vmem, vmem],
        out_specs=(vmem, vmem),
        scratch_shapes=[
            pltpu.VMEM((2, 128, 8192), F32),
            pltpu.VMEM((2, 128, 8192 + NY), BF),
            pltpu.VMEM((2, 3, 128, XROWS * NY), BF),
            pltpu.VMEM((ELECTRODES, 4 * SLAB + 2 * OWN), BF),
            pltpu.VMEM((2, ELECTRODES, ELECTRODES), BF),
            pltpu.VMEM((2, ELECTRODES, ELECTRODES), BF),
            pltpu.VMEM((2, 2, 256, 256), F32),
            pltpu.VMEM((2, ELECTRODES, 2 * NY), F32),
            pltpu.VMEM((2,) + tile, F32),
            pltpu.VMEM((4,) + tile, F32),
            pltpu.VMEM((4,) + tile, F32),
            pltpu.VMEM((4,) + tile, F32),
            pltpu.VMEM(tile, F32),
            pltpu.VMEM(tile, F32),
            pltpu.VMEM((2,) + tile, F32),
            pltpu.VMEM((4,) + tile, F32),
            pltpu.VMEM((2, 2) + tile, F32),
            pltpu.VMEM((17, 2) + tile, F32),
            dma((2, 4)), dma((2, 4)), dma((2, 4, 2)), dma((2, 4, 2)), dma((2, 4, 3, 4)), dma((2, 4, 3, 4)), dma((4,)), dma((4,)),
            dma((2, 4)), dma((2, 4)), dma((2, 4)), dma((2, 4)), dma((2,)), dma((2,)), dma((16,)), dma((16,)), dma((3,)), dma((3,)),
        ],
        compiler_params=pltpu.CompilerParams(collective_id=0, has_side_effects=True, vmem_limit_bytes=60 << 20),
        name="misfit_gradient",
    )(potentials, measurements.T, residuals, conductivity, inside)

    def hand_out(gradient, scaled, gradient_out, scaled_out):
        gradient_out[...] = gradient[...]
        scaled_out[...] = scaled[...]

    return pl.pallas_call(hand_out, out_shape=(shape, shape), in_specs=[vmem, vmem], out_specs=(vmem, vmem), name="hand_out")(*results)


def solution(mesh):
    return jax.shard_map(
        per_device,
        mesh=mesh,
        in_specs=(P("space", "elec", None), P(), P(), P("space", "elec"), P("space", "elec")),
        out_specs=(P(None, "space", "elec"), P(None, "space", "elec")),
        check_vma=False,
    )
```

time: 92.7 us -> 86.9 us (0.937)
  Pallas kernels: 89.1 us -> 85.7 us
  local copies, waits for them, and re-layouts: 2.65 us -> 0 us
    pallas_call x1, Pallas kernels: 89.1 us -> 84.3 us  [per_device(): pl.pallas_call(kernel_body, out_shape=(shape, shape), in_specs=[pl.BlockS...]
    unnamed x2 -> x0, local copies, waits for them, and re-layouts: 2.65 us -> none
    pallas_call x0 -> x1, Pallas kernels: none -> 1.35 us  [per_device(): pl.pallas_call(hand_out, out_shape=(shape, shape), in_specs=[vmem, vmem],...]
where the time goes in v2:
time: 86.9 us; the launch traced here: 86.3 us
  Pallas kernels  85.7 us (99%)
    pallas_call x1, Pallas kernels, per_device(): pl.pallas_call(kernel_body, out_shape=(shape, shape), in_specs=[pl.BlockS...  84.3 us

profile of v2, /device:TPU:33, one launch (start us, length us, event | category | flops | bytes accessed | tf_op | source)
XLA Modules:
  0.0 86.3 jit_solution(12850358194558532854)
XLA Ops:
  0.6 84.3 %misfit_gradient.1 = (f32[2,2,1024]{2,1,0:T(2,128)}, f32[2,2,1024]{2,1,0:T(2,128)}) custom-call(f32[2,128,8192]{2,1,0:T(8,128)} %pot.1, s32[4,16384]{1,0:T(4,128)} %bitcast.1, f32[2,16384]{1,0:T(2,128)} %resid.1, f32[2,1024]{1,0:T(2,128)} %cond.1, s32[2,1024]{1,0:T(2,128)} %inside.1), custom_call_target="tpu_custom_call" | custom-call | tf_op jit(solution)/shard_map/misfit_gradient/pallas_call | solution.py:503
  85.0 1.3 %hand_out.1 = (f32[2,2,1024]{2,1,0:T(2,128)}, f32[2,2,1024]{2,1,0:T(2,128)}) custom-call(f32[2,2,1024]{2,1,0:T(2,128)} %get-tuple-element.4.gradient, f32[2,2,1024]{2,1,0:T(2,128)} %get-tuple-element.5.scaled), custom_call_target="tpu_custom_call" | custom-call | tf_op jit(solution)/shard_map/hand_out/pallas_call | solution.py:538

commit v3 on v2

--- a/solution.py
+++ b/solution.py
@@ -17,7 +17,7 @@
 F32 = jnp.float32
 QUAD_CHUNK = 2048
 XROWS = 4 * ROWS + 1
-GROUP = 256
+GROUP = 512
 ADJ_ROWS = 1024
 ZCOL = 4 * SLAB
 
@@ -128,7 +128,7 @@
     def y_start(p, d, h=0):
         for m, piece in enumerate(pieces(p, d)):
             if piece[0] == h:
-                for dy in (1, 3, 2):
+                for dy in (2, 1, 3):
                     y_copy(p, d, m, dy).start()
         if d == 0 or h == len(x_parts()) - 1:
             local_copy(p, d).start()
@@ -154,7 +154,7 @@
                 cols = pl.ds(q * quarter, quarter)
                 send[p, rows, cols] = stage[p, rows, cols].astype(BF)
                 return 0
-            lax.fori_loop(0, 8, cast, 0)
+            lax.fori_loop(0, 8, cast, 0, unroll=8)
         if p == 0:
             pl.semaphore_wait(bar, 22 + targets)
         for d in (1, 3, 2):

time: 86.9 us -> 86.8 us (level); the launches traced: 86.3 us -> 85.3 us
  Pallas kernels: 85.7 us -> 84.6 us
    pallas_call x1, Pallas kernels: 84.3 us -> 83.3 us  [per_device(): pl.pallas_call(kernel_body, out_shape=(shape, shape), in_specs=[pl.BlockS...]
where the time goes in v3:
time: 86.8 us; the launch traced here: 85.3 us
  Pallas kernels  84.6 us (97%)
    pallas_call x1, Pallas kernels, per_device(): pl.pallas_call(kernel_body, out_shape=(shape, shape), in_specs=[pl.BlockS...  83.3 us

profile of v3, /device:TPU:33, one launch (start us, length us, event | category | flops | bytes accessed | tf_op | source)
XLA Modules:
  0.0 85.3 jit_solution(7510999219932649276)
XLA Ops:
  0.6 83.3 %misfit_gradient.1 = (f32[2,2,1024]{2,1,0:T(2,128)}, f32[2,2,1024]{2,1,0:T(2,128)}) custom-call(f32[2,128,8192]{2,1,0:T(8,128)} %pot.1, s32[4,16384]{1,0:T(4,128)} %bitcast.1, f32[2,16384]{1,0:T(2,128)} %resid.1, f32[2,1024]{1,0:T(2,128)} %cond.1, s32[2,1024]{1,0:T(2,128)} %inside.1), custom_call_target="tpu_custom_call" | custom-call | tf_op jit(solution)/shard_map/misfit_gradient/pallas_call | solution.py:503
  83.9 1.3 %hand_out.1 = (f32[2,2,1024]{2,1,0:T(2,128)}, f32[2,2,1024]{2,1,0:T(2,128)}) custom-call(f32[2,2,1024]{2,1,0:T(2,128)} %get-tuple-element.4.gradient, f32[2,2,1024]{2,1,0:T(2,128)} %get-tuple-element.5.scaled), custom_call_target="tpu_custom_call" | custom-call | tf_op jit(solution)/shard_map/hand_out/pallas_call | solution.py:538
